TPU v7x, 32 devices: a whole 2x2x4 slice. The times are simulated.
32 devices in a mesh: rows: 8 (over y, x, core), tok: 4 (over z).
Axes of the slice: x: 2, y: 2, z: 4, core: 2. Of those that a mesh axis runs over, the one named last changes fastest.
Arguments:
- pixels: bfloat16 [1024, 425, 512], P('rows', None, 'tok'), as said below
- scene_starts: int32 [4], replicated, may hold values from 0 to 960, as said below
- owners: int32 [256, 128], P('rows', 'tok'), may hold values from 0 to 7, as said below
- start_basis: float32 [425, 64], replicated, may hold values from -6 to 6
Outputs:
- tokens: bfloat16 [32768, 1024], P(('rows', 'tok'))
- noise_scores: bfloat16 [1024, 64, 512], P('rows', None, 'tok')
Inputs may be any that keep to these rules, and one draw needn't show every extreme that they name: `scene_starts`: entry 0 is 0 and the entries rise strictly. `owners`: in each block of 32 x 128/4 patches every owner appears exactly 128 times. `pixels`: finite radiances; the scenes have a positive mean.
All inputs are finite; a program needn't handle non-finite values. Where the computation divides by a largest or mean magnitude, that divisor is 1e-20 or more.
Results may differ from a plain program's by a relative error of at most 0.0068.
Values may be sent and summed in bfloat16 or wider, within the bound.
A program may use at most 192 MiB of HBM per device.

v0:
```python
import jax
import jax.numpy as jnp
from jax import lax
from jax.sharding import PartitionSpec as P

PS = 4
NS_ITERS = 10
SUB_ITERS = 2


def passed_along(value, axis, steps):
    count = lax.axis_size(axis)
    leading, last = (max(0, -steps), min(count, count - steps))
    return lax.ppermute(value, axis, [(source, source + steps) for source in range(leading, last)])


def product(left, right):
    return jnp.dot(left, right, precision=lax.Precision.HIGHEST)


def whiten(noise_cov):
    width = noise_cov.shape[0]
    scale = jnp.max(jnp.sum(jnp.abs(noise_cov), axis=1))
    identity = jnp.eye(width, dtype=jnp.float32)
    upper = noise_cov / scale
    lower = identity
    for repeat in range(NS_ITERS):
        middle = 1.5 * identity - 0.5 * product(lower, upper)
        upper = product(upper, middle)
        lower = product(middle, lower)
    return lower / jnp.sqrt(scale)


def orthonormal(block):
    gram = product(block.T, block)
    factor = jnp.linalg.cholesky(gram)
    return lax.linalg.triangular_solve(factor, block, left_side=False, lower=True, transpose_a=True)


def second_moment(block):
    return jnp.einsum("rbc,rec->be", block, block, preferred_element_type=jnp.float32)


def local(pixels, scene_starts, owners, start_basis):
    row_count = lax.axis_size("rows")
    local_rows, bands, local_cols = pixels.shape
    total_rows = local_rows * row_count
    total_cols = local_cols * lax.axis_size("tok")
    scenes = scene_starts.shape[0]
    first_row = passed_along(pixels[0:1], "rows", -1)
    following = jnp.concatenate([pixels[1:], first_row], axis=0)
    global_row = lax.axis_index("rows") * local_rows + jnp.arange(local_rows, dtype=jnp.int32)
    successor = global_row + 1
    starting = jnp.any(successor[:, None] == scene_starts[None, :], axis=1)
    valid = jnp.logical_and(successor < total_rows, jnp.logical_not(starting))
    differ = jnp.where(
        valid[:, None, None], pixels.astype(jnp.float32) - following.astype(jnp.float32), 0.0
    )
    differ = differ.astype(jnp.bfloat16)
    noise_norm = jnp.float32(2 * (total_rows - scenes) * total_cols)
    pixel_total = jnp.float32(total_rows * total_cols)
    noise_local = second_moment(differ)
    signal_local = second_moment(pixels)
    band_local = jnp.sum(pixels, axis=(0, 2), dtype=jnp.float32)
    noise_sum, signal_sum, band_sum = lax.psum(
        (noise_local, signal_local, band_local), ("rows", "tok")
    )
    whitener = whiten(noise_sum / noise_norm)
    pixel_mean = band_sum / pixel_total
    signal_cov = signal_sum / pixel_total - pixel_mean[:, None] * pixel_mean[None, :]
    whitened = product(product(whitener, signal_cov), whitener)
    basis = orthonormal(start_basis)
    for repeat in range(SUB_ITERS):
        basis = orthonormal(product(whitened, basis))
    projector = product(whitener, basis).astype(jnp.bfloat16)
    offset = product(pixel_mean, projector.astype(jnp.float32))
    components = jnp.einsum("bk,rbc->rkc", projector, pixels, preferred_element_type=jnp.float32)
    components = (components - offset[None, :, None]).astype(jnp.bfloat16)
    noise_scores = jnp.einsum(
        "bk,rbc->rkc", projector, differ, preferred_element_type=jnp.float32
    ).astype(jnp.bfloat16)
    comps = components.shape[1]
    rows_per = local_rows // PS
    cols_per = local_cols // PS
    patch_count = rows_per * cols_per
    token_width = PS * PS * comps
    patch_tokens = components.reshape(rows_per, PS, comps, cols_per, PS).transpose(0, 3, 1, 4, 2)
    patch_tokens = patch_tokens.reshape(patch_count, token_width)
    patch_owner = owners.reshape(patch_count)
    per_owner = patch_count // row_count
    one_hot = (patch_owner[:, None] == jnp.arange(row_count, dtype=jnp.int32)[None, :]).astype(
        jnp.int32
    )
    running = jnp.cumsum(one_hot, axis=0) - 1
    rank = jnp.sum(running * one_hot, axis=1)
    position = patch_owner * per_owner + rank
    order = (
        jnp.zeros((patch_count,), jnp.int32)
        .at[position]
        .set(jnp.arange(patch_count, dtype=jnp.int32))
    )
    outgoing = patch_tokens[order].reshape(row_count, per_owner, token_width)
    arrived = lax.all_to_all(outgoing, "rows", split_axis=0, concat_axis=0, tiled=True)
    tokens = arrived.reshape(patch_count, token_width)
    return (tokens, noise_scores)


def solution(mesh):
    placed = (P("rows", None, "tok"), P(), P("rows", "tok"), P())
    return jax.shard_map(
        local,
        mesh=mesh,
        in_specs=placed,
        out_specs=(P(("rows", "tok"), None), P("rows", None, "tok")),
        check_vma=False,
    )
```

profile of v0, /device:TPU:0, one launch (start us, length us, event | category | flops | bytes accessed | tf_op | source)
XLA Modules:
  0.0 430.5 jit_solution(13199155706940572021)
XLA Ops:
  7.2 1.3 slice.24
  8.6 1.3 collective-permute-start
  9.9 15.5 %slice.18 = bf16[127,425,128]{2,0,1:T(8,128)(2,1)} slice(bf16[128,425,128]{2,0,1:T(8,128)(2,1)} %param.7), slice={[1:128], [0:425], [0:128]} | slice | bytes 27635200 | tf_op jit(solution)/shard_map/slice | solution.py:51
  25.4 18.7 %copy.40 = bf16[128,425,128]{0,1,2:T(8,128)(2,1)} copy(bf16[128,425,128]{2,0,1:T(8,128)(2,1)} %param.7) | data formatting | bytes 27852800 | tf_op args[0]
  44.4 16.3 %convolution_bitcast_fusion = f32[425,425]{1,0:T(8,128)} fusion(bf16[128,425,128]{0,1,2:T(8,128)(2,1)} %copy.40), kind=kOutput, calls=%fused_computation.21 | convolution fusion | flops 5918720000 | bytes 14648900 | tf_op jit(solution)/shard_map/rbc,rec->be/dot_general | solution.py:41
  61.0 5.8 %cholesky.59 = f32[64,64]{1,0:T(8,128)S(1)} custom-call(f32[64,64]{1,0:T(8,128)S(1)} %fusion.28), custom_call_target="Cholesky" | custom-call | tf_op jit(solution)/shard_map/jit(cholesky)/cholesky | solution.py:36
  67.5 0.7 fusion.18
  68.3 2.3 reduce-window.6
  71.3 20.2 %fusion.1 = (bf16[128,425,128]{2,0,1:T(8,128)(2,1)}, f32[425]{0:T(512)S(1)}) fusion(bf16[128,425,128]{2,0,1:T(8,128)(2,1)} %param.7, bf16[1,425,128]{2,0,1:T(2,128)(2,1)S(1)} %copy.37, bf16[127,425,128]{2,0,1:T(8,128)(2,1)} %slice.18, pred[128]{0:T(512)(128)(4,1)S(1)} %not_and_fusion), kind=kLoop, calls=%fused_computation.5 | loop fusion | flops 62668376 | bytes 41781028 | tf_op jit(solution)/shard_map/convert_element_type | solution.py:59
  91.5 18.7 %copy.38 = bf16[128,425,128]{0,1,2:T(8,128)(2,1)} copy(bf16[128,425,128]{2,0,1:T(8,128)(2,1)} %get-tuple-element.6) | data formatting | bytes 27852800 | tf_op jit(solution)/shard_map/convert_element_type | solution.py:59
  110.2 26.4 %convolution_bitcast_fusion.1 = f32[425,425]{1,0:T(8,128)} fusion(bf16[128,425,128]{0,1,2:T(8,128)(2,1)} %copy.38), kind=kOutput, calls=%fused_computation.22 | convolution fusion | flops 5918720000 | bytes 14648900 | tf_op jit(solution)/shard_map/rbc,rec->be/dot_general | solution.py:41
  136.6 4.9 %custom-call.7 = f32[1,64,64]{1,2,0:T(8,128)S(1)} custom-call(f32[1,64,64]{2,1,0:T(8,128)S(1)} %fusion.18), custom_call_target="InvertDiagBlocksLowerTriangular" | custom-call | tf_op jit(solution)/shard_map/triangular_solve/custom-call.0 | solution.py:37
  141.5 4.3 %scatter_custom_fusion = s32[1024]{0:T(1024)S(1)} fusion(s32[1024]{0:T(1024)S(1)} %bitcast.155, s32[1024]{0:T(1024)S(1)} %iota.104, s32[]{:T(128)} %constant.70.clone.1), kind=kCustom, calls=%fused_computation.87 | custom fusion | bytes 4100 | tf_op jit(solution)/shard_map/scatter | solution.py:100
  146.2 42.7 %psum.23 = f32[425]{0:T(512)S(1)} all-reduce(f32[425]{0:T(512)S(1)} %get-tuple-element.7), channel_id=1, replica_groups=mesh['rows'=8,'tok'=4] {'rows','tok'}, use_global_device_ids=true, to_apply=%region_6.7 | all-reduce | flops 425 | bytes 3400 | tf_op jit(solution)/shard_map/psum | solution.py:65
  188.9 83.9 %all-reduce.3.cloned.1.call-done = (f32[425,425]{1,0:T(8,128)}, f32[425,425]{1,0:T(8,128)}) async-done(((f32[425,425]{1,0:T(8,128)}, f32[425,425]{1,0:T(8,128)}), (f32[425,425]{1,0:T(8,128)}, f32[425,425]{1,0:T(8,128)})) %all-reduce.3.cloned.1.call-update) | async-done | bytes 1445016 | tf_op jit(solution)/shard_map/psum | solution.py:65
  272.9 1.4 abs_reduce_fusion
  274.8 2.8 select_subtract_fusion.9
  277.6 0.8 fusion.11
  278.5 3.5 fusion.15
  281.9 1.6 select_subtract_fusion.8
  283.5 1.6 fusion.41
  285.1 1.6 fusion.42
  286.7 1.6 select_subtract_fusion.7
  288.3 1.6 fusion.43
  289.9 2.0 fusion.44
  291.9 1.6 select_subtract_fusion.6
  293.5 1.6 fusion.45
  295.1 1.6 fusion.46
  296.7 1.6 select_subtract_fusion.5
  298.3 1.6 fusion.47
  299.9 1.6 fusion.48
  301.5 1.6 select_subtract_fusion.4
  303.1 1.8 fusion.49
  304.9 1.6 fusion.50
  306.4 1.6 select_subtract_fusion.3
  308.1 1.6 fusion.51
  309.6 1.6 fusion.52
  311.2 1.6 select_subtract_fusion.2
  312.8 1.6 fusion.53
  314.4 1.6 fusion.54
  316.0 1.6 select_subtract_fusion.1
  317.6 1.8 fusion.55
  319.4 1.6 fusion.56
  321.7 1.6 select_subtract_fusion
  323.3 1.6 convolution_divide_fusion
  324.9 1.7 fusion.7
  326.7 1.6 fusion.57
  328.3 0.9 fusion.59
  329.6 5.8 %cholesky.70 = f32[64,64]{1,0:T(8,128)S(1)} custom-call(f32[64,64]{1,0:T(8,128)S(1)} %fusion.26), custom_call_target="Cholesky" | custom-call | tf_op jit(solution)/shard_map/jit(cholesky)/cholesky | solution.py:36
  336.1 0.7 fusion.19
  336.8 4.9 %custom-call.8 = f32[1,64,64]{1,2,0:T(8,128)S(1)} custom-call(f32[1,64,64]{2,1,0:T(8,128)S(1)} %fusion.19), custom_call_target="InvertDiagBlocksLowerTriangular" | custom-call | tf_op jit(solution)/shard_map/triangular_solve/custom-call.0 | solution.py:37
  342.0 1.3 fusion.61
  343.7 5.8 %cholesky.81 = f32[64,64]{1,0:T(8,128)S(1)} custom-call(f32[64,64]{1,0:T(8,128)S(1)} %fusion.24), custom_call_target="Cholesky" | custom-call | tf_op jit(solution)/shard_map/jit(cholesky)/cholesky | solution.py:36
  350.9 4.9 %custom-call.9 = f32[1,64,64]{1,2,0:T(8,128)S(1)} custom-call(f32[1,64,64]{2,1,0:T(8,128)S(1)} %fusion.20), custom_call_target="InvertDiagBlocksLowerTriangular" | custom-call | tf_op jit(solution)/shard_map/triangular_solve/custom-call.0 | solution.py:37
  356.1 0.9 convolution_convert_fusion
  357.2 13.4 %fusion.6 = bf16[128,64,128]{2,1,0:T(8,128)(2,1)S(1)} fusion(f32[64]{0:T(128)S(1)} %convolution_bitcast_fusion.5, bf16[425,64]{0,1:T(8,128)(2,1)S(1)} %convolution_convert_fusion, bf16[128,425,128]{2,0,1:T(8,128)(2,1)} %param.7), kind=kOutput, calls=%fused_computation.20 | convolution fusion | flops 893386752 | bytes 16078208 | tf_op jit(solution)/shard_map/bk,rbc->rkc/dot_general | solution.py:77
  370.6 3.3 copy.46
  374.0 5.9 %copy.47 = bf16[32,32,4,4,64]{4,3,2,1,0:T(4,128)(2,1)} copy(bf16[32,32,4,4,64]{4,3,1,2,0:T(4,128)(2,1)} %bitcast.149) | data formatting | bytes 4194304 | tf_op jit(solution)/shard_map/transpose | solution.py:87
  379.9 6.7 %reshape.95 = bf16[1024,1024]{1,0:T(8,128)(2,1)S(1)} reshape(bf16[32,32,4,4,64]{4,3,2,1,0:T(4,128)(2,1)} %copy.47) | data formatting | bytes 4194304 | tf_op jit(solution)/shard_map/reshape | solution.py:88
  386.6 5.3 %gather_fusion = bf16[1024,1024]{1,0:T(8,128)(2,1)} fusion(bf16[1024,1024]{1,0:T(8,128)(2,1)S(1)} %reshape.95, s32[1024]{0:T(1024)S(1)} %fusion.34), kind=kCustom, calls=%fused_computation | custom fusion | bytes 4198400 | tf_op jit(solution)/shard_map/gather | solution.py:102
  391.9 3.6 all-to-all-start
  395.5 14.8 %convert_bitcast_fusion = bf16[128,64,128]{2,1,0:T(8,128)(2,1)} fusion(bf16[128,425,128]{2,0,1:T(8,128)(2,1)} %get-tuple-element.6, bf16[425,64]{0,1:T(8,128)(2,1)S(1)} %convolution_convert_fusion), kind=kOutput, calls=%fused_computation.19 | convolution fusion | flops 892338176 | bytes 16077952 | tf_op jit(solution)/shard_map/bk,rbc->rkc/dot_general | solution.py:79
  410.3 11.8 %all-to-all-done = bf16[8,128,1024]{2,1,0:T(8,128)(2,1)S(1)} async-done(((bf16[8,128,1024]{2,1,0:T(8,128)(2,1)}), bf16[8,128,1024]{2,1,0:T(8,128)(2,1)S(1)}, u32[]{:S(2)}, u32[]{:S(2)}) %all-to-all-start) | async-done | bytes 2097184 | tf_op jit(solution)/shard_map/all_to_all | solution.py:103
  422.1 1.3 copy.61
  (50 shorter events, 6.6 us)
Async XLA Ops:
  7.2 53.5 %copy-start = (f32[425,64]{0,1:T(8,128)S(1)}, f32[425,64]{0,1:T(8,128)}, u32[]{:S(2)}) copy-start(f32[425,64]{0,1:T(8,128)} %param.10) | copy-start | bytes 326404
  7.2 265.7 %all-reduce.3.cloned.1.call-start = ((), (), s32[]{:S(2)}) async-start(), calls=%async_computation.1 | async-start | bytes 3538944 | tf_op jit(solution)/shard_map/psum | solution.py:65
  8.6 62.6 %collective-permute-start = (bf16[1,425,128]{2,1,0:T(8,128)(2,1)S(1)}, bf16[1,425,128]{2,1,0:T(8,128)(2,1)S(1)}, u32[]{:S(2)}, u32[]{:S(2)}) collective-permute-start(bf16[1,425,128]{2,1,0:T(8,128)(2,1)S(1)} %copy.57), channel_id=1, source_target_pairs={{4,0},{8,4},{12,8},{16,12},{20,16},{24,20},{28,24},{5,1},{9,5},{13... | collective-permute-start | bytes 326408 | tf_op jit(solution)/shard_map/ppermute | solution.py:14
  25.4 18.8 %copy-start.2 = (s32[32,32]{1,0:T(8,128)S(1)}, s32[32,32]{1,0:T(8,128)}, u32[]{:S(2)}) copy-start(s32[32,32]{1,0:T(8,128)} %param.9) | copy-start | bytes 12292
  25.4 18.9 %copy-start.3 = (s32[4]{0:T(128)S(1)}, s32[4]{0:T(128)}, u32[]{:S(2)}) copy-start(s32[4]{0:T(128)} %param.8) | copy-start | bytes 52
  308.0 16.9 %copy-start.1 = (f32[425,425]{1,0:T(8,128)S(1)}, f32[425,425]{1,0:T(8,128)}, u32[]{:S(2)}) copy-start(f32[425,425]{1,0:T(8,128)} %get-tuple-element.5) | copy-start | bytes 2167504
  391.9 30.2 %all-to-all-start = ((bf16[8,128,1024]{2,1,0:T(8,128)(2,1)}), bf16[8,128,1024]{2,1,0:T(8,128)(2,1)S(1)}, u32[]{:S(2)}, u32[]{:S(2)}) async-start(bf16[8,128,1024]{2,1,0:T(8,128)(2,1)} %bitcast.150), calls=%async_computation | async-start | bytes 4194304 | tf_op jit(solution)/shard_map/all_to_all | solution.py:103
Sparse Core Ops, SparseCore 0:
  136.7 136.1 all-reduce.2
where the time goes:
time: 436 us; the launch traced here: 430 us
  matrix products  128 us (29%)
  waiting for transfers between devices  95.8 us (22%)
  local copies, waits for them, and re-layouts  82.1 us (19%)
  other arithmetic  61 us (14%)
  blocking collectives  42.7 us (10%)
  between operations  15.4 us (4%)
  starting transfers between devices  4.93 us (1%)
    psum x1, waiting for transfers between devices, local(): lax.psum((noise_local, signal_local, band_local), ('rows', 'tok'))  83.9 us
    dot_general x38, matrix products, product(): return jnp.dot(left, right, precision=lax.Precision.HIGHEST)  56.6 us
    psum x1, blocking collectives, local(): lax.psum((noise_local, signal_local, band_local), ('rows', 'tok'))  42.7 us
    dot_general x2, matrix products, second_moment(): jnp.einsum('rbc,rec->be', block, block, preferred_element_type=jnp.float32)  42.6 us
    convert_element_type x1, other arithmetic, local(): differ = differ.astype(jnp.bfloat16)  20.2 us
    unnamed x11, local copies, waits for them, and re-layouts  20.1 us
    another operation x9, other arithmetic, orthonormal(): factor = jnp.linalg.cholesky(gram)  19.6 us
    convert_element_type x1, local copies, waits for them, and re-layouts, local(): differ = differ.astype(jnp.bfloat16)  18.7 us
  transfers between devices with their start and end apart: 3, of which 2 were waited for; matrix products, arithmetic and copies ran while one was open for 20% of the time, Pallas kernels for 0%

commit v1 on v0

v1 whole, which is shorter than its diff:
```python
import functools

import jax
import jax.numpy as jnp
from jax import lax
from jax.experimental import pallas as pl
from jax.experimental.pallas import tpu as pltpu
from jax.sharding import PartitionSpec as P

PS = 4
NS_ITERS = 10
STEP = 16
HALF = 256
F32 = jnp.float32
BF16 = jnp.bfloat16
NT = (((1,), (1,)), ((), ()))


def up(value, unit):
    return -(-value // unit) * unit


def passed_along(value, axis, steps):
    count = lax.axis_size(axis)
    leading, last = (max(0, -steps), min(count, count - steps))
    return lax.ppermute(value, axis, [(source, source + steps) for source in range(leading, last)])


def moments_kernel(x_ref, ahead_ref, halo_ref, valid_ref, wide_ref, tail_ref, band_ref, xs, ds, total):
    step = pl.program_id(0)
    steps = pl.num_programs(0)
    rows, bands, cols = x_ref.shape
    tall = xs.shape[0]

    @pl.when(step == 0)
    def _():
        wide_ref[...] = jnp.zeros_like(wide_ref)
        tail_ref[...] = jnp.zeros_like(tail_ref)
        total[...] = jnp.zeros_like(total)
        xs[...] = jnp.zeros_like(xs)
        ds[...] = jnp.zeros_like(ds)

    last = step == steps - 1
    here = x_ref[0].astype(F32)
    sums = total[...]
    for r in range(rows):
        if r + 1 < rows:
            after = x_ref[r + 1].astype(F32)
        else:
            after = jnp.where(last, halo_ref[0], ahead_ref[0]).astype(F32)
        keep = valid_ref[step * rows + r] != 0
        at = slice(r * cols, (r + 1) * cols)
        xs[0:bands, at] = x_ref[r]
        ds[0:bands, at] = jnp.where(keep, here - after, 0.0).astype(BF16)
        sums = sums + here
        here = after
    total[...] = sums
    for index, ref in enumerate((ds, xs)):
        wide_ref[index] += lax.dot_general(
            ref[...], ref[0:HALF, :], NT, preferred_element_type=F32
        )
        tail_ref[index] += lax.dot_general(
            ref[HALF:tall, :], ref[HALF:tall, :], NT, preferred_element_type=F32
        )

    @pl.when(last)
    def _():
        band_ref[...] = jnp.zeros_like(band_ref)
        band_ref[0:bands, :] = jnp.sum(total[...], axis=1, keepdims=True)


def moments(pixels, halo, valid):
    local_rows, bands, cols = pixels.shape
    tall = up(bands, 16)
    steps = local_rows // STEP
    last_row = local_rows - 1
    return pl.pallas_call(
        moments_kernel,
        grid=(steps,),
        in_specs=[
            pl.BlockSpec((STEP, bands, cols), lambda i: (i, 0, 0)),
            pl.BlockSpec((1, bands, cols), lambda i: (jnp.minimum((i + 1) * STEP, last_row), 0, 0)),
            pl.BlockSpec((1, bands, cols), lambda i: (0, 0, 0)),
            pl.BlockSpec(memory_space=pltpu.SMEM),
        ],
        out_specs=[
            pl.BlockSpec((2, tall, HALF), lambda i: (0, 0, 0)),
            pl.BlockSpec((2, tall - HALF, tall - HALF), lambda i: (0, 0, 0)),
            pl.BlockSpec((tall, 1), lambda i: (0, 0)),
        ],
        out_shape=[
            jax.ShapeDtypeStruct((2, tall, HALF), F32),
            jax.ShapeDtypeStruct((2, tall - HALF, tall - HALF), F32),
            jax.ShapeDtypeStruct((tall, 1), F32),
        ],
        scratch_shapes=[
            pltpu.VMEM((tall, STEP * cols), BF16),
            pltpu.VMEM((tall, STEP * cols), BF16),
            pltpu.VMEM((bands, cols), F32),
        ],
        compiler_params=pltpu.CompilerParams(vmem_limit_bytes=48 * 2**20),
        cost_estimate=pl.CostEstimate(
            flops=4 * local_rows * cols * bands * bands,
            bytes_accessed=2 * local_rows * cols * bands,
            transcendentals=0,
        ),
        name="moments",
    )(pixels, pixels, halo, valid)


def split(value):
    high = value.astype(BF16)
    return high, (value - high.astype(F32)).astype(BF16)


def dot3(left, right):
    (lh, ll), (rh, rl) = left, right
    dot = functools.partial(jnp.dot, preferred_element_type=F32)
    return dot(lh, rh) + (dot(ll, rh) + dot(lh, rl))


def dot3_nt(left, right):
    (lh, ll), (rh, rl) = left, right
    dot = functools.partial(lax.dot_general, dimension_numbers=NT, preferred_element_type=F32)
    return dot(lh, rh) + (dot(ll, rh) + dot(lh, rl))


def projector_kernel(
    noise_norm, pixel_total, wide_ref, tail_ref, band_ref, start_ref, proj_ref, offset_ref,
    full, uh, ul, lh, ll, mh, ml, sh, sl,
):
    size = full.shape[0]
    tall = wide_ref.shape[1]
    bands = proj_ref.shape[1]
    comps = proj_ref.shape[0]
    rows = lax.broadcasted_iota(jnp.int32, (size, size), 0)
    lanes = lax.broadcasted_iota(jnp.int32, (size, size), 1)
    eye = jnp.where(rows == lanes, 1.0, 0.0).astype(F32)[0:tall]

    def assemble(index):
        full[...] = jnp.zeros_like(full)
        full[0:tall, 0:HALF] = wide_ref[index]
        full[HALF:tall, HALF:tall] = tail_ref[index]
        full[0:HALF, HALF:size] = full[HALF:size, 0:HALF].T
        return full[0:tall, :]

    def put(high, low, value):
        high[0:tall, :], low[0:tall, :] = split(value)

    for ref in (uh, ul, lh, ll, mh, ml, sh, sl):
        ref[...] = jnp.zeros_like(ref)
    band = jnp.broadcast_to(band_ref[...], (tall, 128)) / pixel_total
    band = jnp.concatenate([band, jnp.zeros((size - tall, 128), F32)], axis=0)
    mean_col = band[0:tall, 0:1]
    mean_row = band.T[0:1, :]
    put(sh, sl, assemble(1) / pixel_total - mean_col * mean_row)

    noise_cov = assemble(0) / noise_norm
    scale = jnp.max(jnp.sum(jnp.abs(noise_cov), axis=1, keepdims=True), axis=0, keepdims=True)
    upper = noise_cov / scale
    put(uh, ul, upper)
    middle = 1.5 * eye - 0.5 * upper
    put(mh, ml, middle)
    put(lh, ll, middle)

    def pair(high, low):
        return high[...], low[...]

    def left(high, low):
        return high[0:tall, :], low[0:tall, :]

    put(uh, ul, dot3(left(uh, ul), pair(mh, ml)))

    def iteration(repeat, carry):
        put(mh, ml, 1.5 * eye - 0.5 * dot3(left(lh, ll), pair(uh, ul)))
        put(uh, ul, dot3(left(uh, ul), pair(mh, ml)))
        put(lh, ll, dot3(left(lh, ll), pair(mh, ml)))
        return carry

    lax.fori_loop(0, NS_ITERS - 2, iteration, 0)
    put(mh, ml, 1.5 * eye - 0.5 * dot3(left(lh, ll), pair(uh, ul)))
    whitener = dot3(left(lh, ll), pair(mh, ml)) * lax.rsqrt(scale)
    put(lh, ll, whitener)

    def whitened(block):
        for high, low in ((lh, ll), (sh, sl), (lh, ll)):
            block = dot3(split(block), pair(high, low))
        return block

    block = whitened(start_ref[...])
    largest = jnp.max(jnp.max(jnp.abs(block), axis=1, keepdims=True), axis=0, keepdims=True)
    block = whitened(block / largest)
    largest = jnp.max(jnp.max(jnp.abs(block), axis=1, keepdims=True), axis=0, keepdims=True)
    block = block / largest
    gram = lax.dot_general(
        block, block, NT, precision=lax.Precision.HIGHEST, preferred_element_type=F32
    )
    k_rows = lax.broadcasted_iota(jnp.int32, (comps, comps), 0)
    k_lanes = lax.broadcasted_iota(jnp.int32, (comps, comps), 1)
    work = jnp.concatenate([gram, jnp.where(k_rows == k_lanes, 1.0, 0.0).astype(F32)], axis=1)
    row_index = lax.broadcasted_iota(jnp.int32, (comps, 2 * comps), 0)
    for j in range(comps):
        pivot_row = work[j:j + 1, :]
        inverse = lax.rsqrt(pivot_row[:, j:j + 1])
        pivot_row = pivot_row * inverse
        factor = work[:, j:j + 1] * inverse
        work = jnp.where(
            row_index > j, work - factor * pivot_row, jnp.where(row_index == j, pivot_row, work)
        )
    basis = jnp.dot(
        work[:, comps:], block, precision=lax.Precision.HIGHEST, preferred_element_type=F32
    )
    projector = dot3(split(basis), pair(lh, ll)).astype(BF16)
    proj_ref[...] = projector[:, 0:bands]
    offset = jnp.sum(projector.astype(F32) * mean_row, axis=1, keepdims=True)
    offset_ref[...] = jnp.broadcast_to(offset, offset_ref.shape)


def make_projector(wide, tail, band, start, noise_norm, pixel_total):
    tall = wide.shape[1]
    comps, size = start.shape[0], up(tall, 128)
    square = pltpu.VMEM((size, size), BF16)
    return pl.pallas_call(
        functools.partial(projector_kernel, noise_norm, pixel_total),
        out_shape=[
            jax.ShapeDtypeStruct((comps, tall), BF16),
            jax.ShapeDtypeStruct((comps, 128), F32),
        ],
        scratch_shapes=[pltpu.VMEM((size, size), F32)] + [square] * 8,
        compiler_params=pltpu.CompilerParams(vmem_limit_bytes=48 * 2**20),
        name="projector",
    )(wide, tail, band, jnp.pad(start, ((0, 0), (0, size - start.shape[1]))))


def project_kernel(
    x_ref, halo_ref, valid_ref, proj_ref, offset_ref, place_ref, spread_ref,
    tokens_ref, scores_ref, ahead, raster,
):
    step = pl.program_id(0)
    steps = pl.num_programs(0)
    block = steps - 1 - step
    rows, bands, cols = x_ref.shape
    comps = proj_ref.shape[0]
    projector = proj_ref[...][:, 0:bands]
    dot = functools.partial(jnp.dot, preferred_element_type=F32)

    @pl.when(step == 0)
    def _():
        ahead[...] = dot(projector, halo_ref[0])

    pixels = jnp.concatenate([x_ref[r] for r in range(rows)], axis=1)
    sums = dot(projector, pixels)
    offset = offset_ref[...]
    after = ahead[...]
    for r in reversed(range(rows)):
        here = sums[:, r * cols:(r + 1) * cols]
        keep = valid_ref[block * rows + r] != 0
        scores_ref[r] = jnp.where(keep, here - after, 0.0).astype(BF16)
        after = here
    ahead[...] = after

    patches = rows // PS
    groups = cols // PS
    chosen_row = lax.broadcasted_iota(jnp.int32, (cols, cols), 0)
    chosen_col = lax.broadcasted_iota(jnp.int32, (cols, cols), 1)
    chosen = jnp.where(
        chosen_col == PS * lax.rem(chosen_row, groups) + lax.div(chosen_row, groups), 1.0, 0.0
    ).astype(BF16)
    columns = []
    for p in range(patches):
        parts = []
        for i in range(PS):
            r = p * PS + i
            parts.append((sums[:, r * cols:(r + 1) * cols] - offset).astype(BF16))
        stacked = jnp.concatenate(parts, axis=0)
        columns.append(
            lax.dot_general(chosen, stacked, NT, preferred_element_type=F32).astype(BF16)
        )
    pair = 2 * comps
    for half in range(PS // 2):
        gathered = jnp.concatenate(
            [
                jnp.concatenate(
                    [
                        part[j * groups:(j + 1) * groups, half * pair:(half + 1) * pair]
                        for j in range(PS)
                    ],
                    axis=1,
                )
                for part in columns
            ],
            axis=0,
        )
        width = PS * pair
        raster[
            pl.ds(pl.multiple_of(block * patches * groups, patches * groups), patches * groups),
            half * width:(half + 1) * width,
        ] = dot(gathered, spread_ref[...]).astype(BF16)

    @pl.when(step == steps - 1)
    def _():
        count = raster.shape[0]
        slots = 256
        tokens = raster[...]
        for first in range(0, count, slots):
            slot = lax.broadcasted_iota(jnp.int32, (slots, count), 0) + first
            chosen_token = jnp.where(slot == place_ref[...], 1.0, 0.0).astype(BF16)
            tokens_ref[first:first + slots, :] = dot(chosen_token, tokens).astype(BF16)


def project(pixels, halo, valid, projector, offset, place, spread):
    local_rows, bands, cols = pixels.shape
    comps = projector.shape[0]
    steps = local_rows // STEP
    patch_count = (local_rows // PS) * (cols // PS)
    width = PS * PS * comps
    return pl.pallas_call(
        project_kernel,
        grid=(steps,),
        in_specs=[
            pl.BlockSpec((STEP, bands, cols), lambda i: (steps - 1 - i, 0, 0)),
            pl.BlockSpec((1, bands, cols), lambda i: (0, 0, 0)),
            pl.BlockSpec(memory_space=pltpu.SMEM),
            pl.BlockSpec(projector.shape, lambda i: (0, 0)),
            pl.BlockSpec(offset.shape, lambda i: (0, 0)),
            pl.BlockSpec(place.shape, lambda i: (0, 0)),
            pl.BlockSpec(spread.shape, lambda i: (0, 0)),
        ],
        out_specs=[
            pl.BlockSpec((patch_count, width), lambda i: (0, 0)),
            pl.BlockSpec((STEP, comps, cols), lambda i: (steps - 1 - i, 0, 0)),
        ],
        out_shape=[
            jax.ShapeDtypeStruct((patch_count, width), BF16),
            jax.ShapeDtypeStruct((local_rows, comps, cols), BF16),
        ],
        scratch_shapes=[
            pltpu.VMEM((comps, cols), F32),
            pltpu.VMEM((patch_count, width), BF16),
        ],
        compiler_params=pltpu.CompilerParams(vmem_limit_bytes=48 * 2**20),
        name="project",
    )(pixels, halo, valid, projector, offset, place, spread)


def local(pixels, scene_starts, owners, start_basis):
    row_count = lax.axis_size("rows")
    local_rows, bands, local_cols = pixels.shape
    total_rows = local_rows * row_count
    total_cols = local_cols * lax.axis_size("tok")
    scenes = scene_starts.shape[0]
    comps = start_basis.shape[1]
    halo = passed_along(pixels[0:1], "rows", -1)
    global_row = lax.axis_index("rows") * local_rows + jnp.arange(local_rows, dtype=jnp.int32)
    successor = global_row + 1
    starting = jnp.any(successor[:, None] == scene_starts[None, :], axis=1)
    valid = jnp.logical_and(successor < total_rows, jnp.logical_not(starting)).astype(jnp.int32)
    noise_norm = float(2 * (total_rows - scenes) * total_cols)
    pixel_total = float(total_rows * total_cols)
    sums = lax.psum(moments(pixels, halo, valid), ("rows", "tok"))
    projector, offset = make_projector(*sums, start_basis.T, noise_norm, pixel_total)

    patch_owner = owners.reshape(-1)
    patch_count = patch_owner.shape[0]
    per_owner = patch_count // row_count
    index = jnp.arange(patch_count, dtype=jnp.int32)
    matches = (patch_owner[None, :] == jnp.arange(row_count, dtype=jnp.int32)[:, None])
    earlier = (index[:, None] < index[None, :]).astype(BF16)
    running = jnp.dot(matches.astype(BF16), earlier, preferred_element_type=F32)
    rank = jnp.sum(jnp.where(matches, running, 0.0), axis=0).astype(jnp.int32)
    place = (patch_owner * per_owner + rank)[None, :]
    source = jnp.arange(2 * comps * PS, dtype=jnp.int32)
    j, within = source // (2 * comps), source % (2 * comps)
    target = (within // comps) * (PS * comps) + j * comps + within % comps
    spread = (target[:, None] == source[None, :]).astype(BF16)

    outgoing, noise_scores = project(pixels, halo, valid, projector, offset, place, spread)
    outgoing = outgoing.reshape(row_count, per_owner, -1)
    arrived = lax.all_to_all(outgoing, "rows", split_axis=0, concat_axis=0, tiled=True)
    return (arrived.reshape(patch_count, -1), noise_scores)


def solution(mesh):
    placed = (P("rows", None, "tok"), P(), P("rows", "tok"), P())
    return jax.shard_map(
        local,
        mesh=mesh,
        in_specs=placed,
        out_specs=(P(("rows", "tok"), None), P("rows", None, "tok")),
        check_vma=False,
    )
```

time: 436 us -> 269 us (0.62); the launches traced: 430 us -> 269 us
  matrix products: 128 us -> 0.32 us
  Pallas kernels: 0 us -> 63.5 us
  other arithmetic: 61 us -> 0.28 us
  local copies, waits for them, and re-layouts: 82.1 us -> 21.8 us
  blocking collectives: 42.7 us -> 77.6 us
  waiting for transfers between devices: 95.8 us -> 89.5 us
    dot_general x42 -> x1, matrix products: 127 us -> 0.32 us  [local(): running = jnp.dot(matches.astype(BF16), earlier, preferred_element_type=F32)]
    pallas_call x0 -> x3, Pallas kernels: none -> 63.5 us  [the longest x1 31.3 us: make_projector(): pl.pallas_call(functools.partial(projector_kernel, noise_norm, pixel_tota...]
    another operation x17 -> x0, other arithmetic: 38.6 us -> none  [the longest x9 19.6 us: orthonormal(): factor = jnp.linalg.cholesky(gram)]
    all_to_all x0 -> x1, blocking collectives: none -> 29.8 us  [local(): lax.all_to_all(outgoing, 'rows', split_axis=0, concat_axis=0, tiled=True)]
    convert_element_type x2 -> x0, local copies, waits for them, and re-layouts: 22.1 us -> none  [the longest x1 18.7 us: local(): differ = differ.astype(jnp.bfloat16)]
    convert_element_type x2 -> x3, other arithmetic: 20.2 us -> 0.17 us  [the longest x1 0.15 us: local(): spread = (target[:, None] == source[None, :]).astype(BF16)]
    slice x2 -> x1, local copies, waits for them, and re-layouts: 16.8 us -> 0.01 us  [local(): halo = passed_along(pixels[0:1], 'rows', -1)]
    all_to_all x1 -> x0, waiting for transfers between devices: 11.8 us -> none  [local(): lax.all_to_all(outgoing, 'rows', split_axis=0, concat_axis=0, tiled=True)]
  transfers between devices with their start and end apart: 3 -> 2, of which waited for: 2 -> 2; matrix products, arithmetic and copies ran while one was open for 20% -> 0% of each run, Pallas kernels for 0% -> 0%
where the time goes in v1:
time: 269 us
  waiting for transfers between devices  89.5 us (33%)
  blocking collectives  77.6 us (29%)
  Pallas kernels  63.5 us (24%)
  local copies, waits for them, and re-layouts  21.8 us (8%)
  between operations  14.2 us (5%)
    psum x1, waiting for transfers between devices, local(): sums = lax.psum(moments(pixels, halo, valid), ('rows', 'tok'))  88.1 us
    psum x1, blocking collectives, local(): sums = lax.psum(moments(pixels, halo, valid), ('rows', 'tok'))  47.8 us
    pallas_call x1, Pallas kernels, make_projector(): pl.pallas_call(functools.partial(projector_kernel, noise_norm, pixel_tota...  31.3 us
    all_to_all x1, blocking collectives, local(): lax.all_to_all(outgoing, 'rows', split_axis=0, concat_axis=0, tiled=True)  29.8 us
    unnamed x14, local copies, waits for them, and re-layouts  21.7 us
    pallas_call x1, Pallas kernels, moments(): pl.pallas_call(moments_kernel, grid=(steps,), in_specs=[pl.BlockSpec((STE...  18 us
    pallas_call x1, Pallas kernels, project(): pl.pallas_call(project_kernel, grid=(steps,), in_specs=[pl.BlockSpec((STE...  14.3 us
  transfers between devices with their start and end apart: 2, of which 2 were waited for; matrix products, arithmetic and copies ran while one was open for 0% of the time, Pallas kernels for 0%

profile of v1, /device:TPU:0, one launch (start us, length us, event | category | flops | bytes accessed | tf_op | source)
XLA Modules:
  0.0 268.6 jit_solution(1864607923514409341)
XLA Ops:
  7.2 0.0 copy-start.5
  7.2 0.0 copy-start.4
  7.2 0.0 all-reduce.4.cloned.1.call-start
  7.2 13.1 %copy.13.x_ref.ahead_ref = bf16[128,425,128]{2,1,0:T(8,128)(2,1)S(1)} copy(bf16[128,425,128]{2,0,1:T(8,128)(2,1)} %param.4) | data formatting | bytes 27852800 | tf_op args[0]
  20.4 0.0 copy-start.2
  20.4 5.1 %copy-done.2 = bf16[128,425,128]{2,1,0:T(8,128)(2,1)} copy-done((bf16[128,425,128]{2,1,0:T(8,128)(2,1)}, bf16[128,425,128]{2,1,0:T(8,128)(2,1)S(1)}, u32[]{:S(2)}) %copy-start.2) | copy-done | bytes 13926424
  25.4 1.3 collective-permute-start
  26.8 0.0 copy-done.5
  26.8 0.1 compare_reduce_fusion
  26.9 0.0 copy-done.4
  26.9 0.1 eq.47
  26.9 0.3 fusion.2
  27.3 0.0 copy-start.3
  27.3 1.4 collective-permute-done.halo_ref
  28.6 18.0 %moments.1 = (f32[2,432,256]{2,1,0:T(8,128)}, f32[2,176,176]{2,1,0:T(8,128)}, f32[432,1]{1,0:T(8,128)S(1)}) custom-call(bf16[128,425,128]{2,1,0:T(8,128)(2,1)} %copy-done.2, bf16[128,425,128]{2,1,0:T(8,128)(2,1)} %copy-done.2, bf16[1,425,128]{2,1,0:T(8,128)(2,1)S(1)} %collective-permute-done.halo_ref, s32[128]{0:T(128)S(1)} %and_convert_fusion.valid_ref), custom_call_target="tpu_custom_call" | custom-call | flops 11837440000 | bytes 13926400 | tf_op jit(solution)/shard_map/moments/pallas_call | solution.py:77
  46.6 0.0 all-reduce.4.cloned.1.call-update
  46.7 0.1 mul.40
  46.7 0.0 copy-done.3
  46.8 0.2 fusion.3.spread_ref
  47.0 47.8 %psum.23.band_ref = f32[432,1]{1,0:T(8,128)S(1)} all-reduce(f32[432,1]{1,0:T(8,128)S(1)} %get-tuple-element.11), channel_id=1, replica_groups=mesh['rows'=8,'tok'=4] {'rows','tok'}, use_global_device_ids=true, to_apply=%region_3.0 | all-reduce | flops 432 | bytes 3456 | tf_op jit(solution)/shard_map/psum | solution.py:360
  94.7 88.1 %all-reduce.4.cloned.1.call-done = (f32[2,432,256]{2,1,0:T(8,128)}, f32[2,176,176]{2,1,0:T(8,128)}) async-done(((f32[2,432,256]{2,1,0:T(8,128)}, f32[2,176,176]{2,1,0:T(8,128)}), (f32[2,432,256]{2,1,0:T(8,128)}, f32[2,176,176]{2,1,0:T(8,128)})) %all-reduce.4.cloned.1.call-update) | async-done | bytes 1132560 | tf_op jit(solution)/shard_map/psum | solution.py:360
  182.8 0.0 copy-start
  182.8 1.2 copy-done
  184.0 0.0 copy-start.1
  184.0 1.0 copy-done.1
  185.0 31.3 %projector.1 = (bf16[64,432]{1,0:T(8,128)(2,1)S(1)}, f32[64,128]{1,0:T(8,128)S(1)}) custom-call(f32[2,432,256]{2,1,0:T(8,128)S(1)} %copy-done, f32[2,176,176]{2,1,0:T(8,128)S(1)} %copy-done.1, f32[432,1]{1,0:T(8,128)S(1)} %psum.23.band_ref, f32[64,512]{1,0:T(8,128)S(1)} %pad.4.start_ref), custom_call_target="tpu_custom_call" | custom-call | tf_op jit(solution)/shard_map/projector/pallas_call | solution.py:223
  216.3 14.3 %project.1 = (bf16[1024,1024]{1,0:T(8,128)(2,1)S(1)}, bf16[128,64,128]{2,1,0:T(8,128)(2,1)}) custom-call(bf16[128,425,128]{2,1,0:T(8,128)(2,1)} %copy-done.2, bf16[1,425,128]{2,1,0:T(8,128)(2,1)S(1)} %collective-permute-done.halo_ref, s32[128]{0:T(128)S(1)} %and_convert_fusion.valid_ref, bf16[64,432]{1,0:T(8,128)(2,1)S(1)} %get-tuple-element.12.proj_ref, ...), custom_call_target="tpu_custom_call" | custom-call | tf_op jit(solution)/shard_map/project/pallas_call | solution.py:317
  230.6 29.8 %all_to_all.5 = bf16[8,128,1024]{2,1,0:T(8,128)(2,1)S(1)} all-to-all(bf16[8,128,1024]{2,1,0:T(8,128)(2,1)S(1)} %bitcast.4), channel_id=1, replica_groups=mesh['rows'=8,'tok'=4] {'rows'}, dimensions={0} | all-to-all | bytes 4194304 | tf_op jit(solution)/shard_map/all_to_all | solution.py:379
  260.4 1.3 copy.17
  (8 shorter events, 0.1 us)
Async XLA Ops:
  7.2 19.6 %copy-start.5 = (s32[4]{0:T(128)S(1)}, s32[4]{0:T(128)}, u32[]{:S(2)}) copy-start(s32[4]{0:T(128)} %param.5) | copy-start | bytes 52
  7.2 19.7 %copy-start.4 = (s32[32,32]{1,0:T(8,128)S(1)}, s32[32,32]{1,0:T(8,128)}, u32[]{:S(2)}) copy-start(s32[32,32]{1,0:T(8,128)} %param.6) | copy-start | bytes 12292
  7.2 175.7 %all-reduce.4.cloned.1.call-start = ((), (), s32[]{:S(2)}) async-start(), calls=%async_computation.1 | async-start | bytes 2490368 | tf_op jit(solution)/shard_map/psum | solution.py:360
  20.4 5.1 %copy-start.2 = (bf16[128,425,128]{2,1,0:T(8,128)(2,1)}, bf16[128,425,128]{2,1,0:T(8,128)(2,1)S(1)}, u32[]{:S(2)}) copy-start(bf16[128,425,128]{2,1,0:T(8,128)(2,1)S(1)} %copy.13.x_ref.ahead_ref) | copy-start | bytes 41779204
  25.4 3.2 %collective-permute-start = (bf16[1,425,128]{2,1,0:T(8,128)(2,1)S(1)}, bf16[1,425,128]{2,1,0:T(8,128)(2,1)S(1)}, u32[]{:S(2)}, u32[]{:S(2)}) collective-permute-start(bf16[1,425,128]{2,1,0:T(8,128)(2,1)S(1)} %slice.4), channel_id=1, source_target_pairs={{4,0},{8,4},{12,8},{16,12},{20,16},{24,20},{28,24},{5,1},{9,5},{13... | collective-permute-start | bytes 326408 | tf_op jit(solution)/shard_map/ppermute | solution.py:26
  27.3 19.5 %copy-start.3 = (f32[425,64]{0,1:T(8,128)S(1)}, f32[425,64]{0,1:T(8,128)}, u32[]{:S(2)}) copy-start(f32[425,64]{0,1:T(8,128)} %param.7) | copy-start | bytes 326404
  182.8 1.2 copy-start
  184.0 1.0 copy-start.1
Sparse Core Ops, SparseCore 0:
  46.8 136.0 all-reduce.3

commit v2 on v1

--- a/solution.py
+++ b/solution.py
@@ -106,6 +106,109 @@
         ),
         name="moments",
     )(pixels, pixels, halo, valid)
+
+
+def exchanges():
+    plan = []
+    for axis in ("rows", "tok"):
+        bit = 1
+        while bit < lax.axis_size(axis):
+            plan.append((axis, bit))
+            bit *= 2
+    return plan
+
+
+def total_kernel(plan, mine_ref, total_ref, held, gathered, *rest):
+    count = len(plan)
+    landing, (send_sem, recv_sem) = rest[:count], rest[count:]
+    partners, bits = [], []
+    for axis, bit in plan:
+        index = lax.axis_index(axis)
+        side = lax.rem(lax.div(index, bit), 2)
+        bits.append(side)
+        place = {"rows": lax.axis_index("rows"), "tok": lax.axis_index("tok")}
+        place[axis] = index + bit * (1 - 2 * side)
+        partners.append((place["rows"], place["tok"]))
+
+    barrier = pltpu.get_barrier_semaphore()
+    for partner in partners:
+        pl.semaphore_signal(
+            barrier, inc=1, device_id=partner, device_id_type=pl.DeviceIdType.MESH
+        )
+    pl.semaphore_wait(barrier, count)
+
+    held[...] = mine_ref[...]
+    base, length = 0, held.shape[0]
+    regions = []
+    for step in range(count):
+        length //= 2
+        keep = pl.multiple_of(base + bits[step] * length, 8)
+        give = pl.multiple_of(base + (1 - bits[step]) * length, 8)
+        copy = pltpu.make_async_remote_copy(
+            src_ref=held.at[pl.ds(give, length)],
+            dst_ref=landing[step],
+            send_sem=send_sem.at[step],
+            recv_sem=recv_sem.at[step],
+            device_id=partners[step],
+            device_id_type=pl.DeviceIdType.MESH,
+        )
+        copy.start()
+        copy.wait()
+        held[pl.ds(keep, length), :] += landing[step][...]
+        regions.append((keep, length))
+        base = keep
+    gathered[pl.ds(base, length), :] = held[pl.ds(base, length), :]
+    for step in reversed(range(count)):
+        keep, length = regions[step]
+        copy = pltpu.make_async_remote_copy(
+            src_ref=gathered.at[pl.ds(keep, length)],
+            dst_ref=gathered.at[pl.ds(keep, length)],
+            send_sem=send_sem.at[count + step],
+            recv_sem=recv_sem.at[count + step],
+            device_id=partners[step],
+            device_id_type=pl.DeviceIdType.MESH,
+        )
+        copy.start()
+        copy.wait()
+    total_ref[...] = gathered[...]
+
+
+def summed(wide, tail, band):
+    plan = exchanges()
+    devices = 2 ** len(plan)
+    tall, half = wide.shape[1:]
+    short = tail.shape[1]
+    flat = jnp.concatenate(
+        [
+            wide.reshape(2 * tall, half),
+            jnp.pad(tail.reshape(2 * short, short), ((0, 0), (0, half - short))),
+            jnp.pad(band.reshape(-1), (0, up(tall, half) - tall)).reshape(-1, half),
+        ],
+        axis=0,
+    )
+    rows = flat.shape[0]
+    full = up(rows, 8 * devices)
+    flat = jnp.pad(flat, ((0, full - rows), (0, 0)))
+    landing = [pltpu.VMEM((full >> (step + 1), half), F32) for step in range(len(plan))]
+    whole = pl.pallas_call(
+        functools.partial(total_kernel, plan),
+        out_shape=jax.ShapeDtypeStruct((full, half), F32),
+        in_specs=[pl.BlockSpec(memory_space=pltpu.VMEM)],
+        out_specs=pl.BlockSpec(memory_space=pltpu.VMEM),
+        scratch_shapes=[pltpu.VMEM((full, half), F32), pltpu.VMEM((full, half), F32)]
+        + landing
+        + [pltpu.SemaphoreType.DMA((2 * len(plan),)), pltpu.SemaphoreType.DMA((2 * len(plan),))],
+        compiler_params=pltpu.CompilerParams(
+            collective_id=0, has_side_effects=True, vmem_limit_bytes=32 * 2**20
+        ),
+        name="total",
+    )(flat)
+    first, second = 2 * tall, 2 * tall + 2 * short
+    return (
+        whole[:first].reshape(2, tall, half),
+        whole[first:second, :short].reshape(2, short, short),
+        whole[second:rows].reshape(-1)[:tall].reshape(tall, 1),
+    )
 
 
 def split(value):
@@ -357,7 +460,7 @@
     valid = jnp.logical_and(successor < total_rows, jnp.logical_not(starting)).astype(jnp.int32)
     noise_norm = float(2 * (total_rows - scenes) * total_cols)
     pixel_total = float(total_rows * total_cols)
-    sums = lax.psum(moments(pixels, halo, valid), ("rows", "tok"))
+    sums = summed(*moments(pixels, halo, valid))
     projector, offset = make_projector(*sums, start_basis.T, noise_norm, pixel_total)
 
     patch_owner = owners.reshape(-1)

time: 269 us -> 166 us (0.62)
  waiting for transfers between devices: 89.5 us -> 1.08 us
  Pallas kernels: 63.5 us -> 112 us
  blocking collectives: 77.6 us -> 30.2 us
  between operations: 14.2 us -> 0.82 us
    psum x1 -> x0, waiting for transfers between devices: 88.1 us -> none  [local(): sums = lax.psum(moments(pixels, halo, valid), ('rows', 'tok'))]
    pallas_call x0 -> x1, Pallas kernels: none -> 49 us  [summed(): pl.pallas_call(functools.partial(total_kernel, plan), out_shape=jax.Shape...]
    psum x1 -> x0, blocking collectives: 47.8 us -> none  [local(): sums = lax.psum(moments(pixels, halo, valid), ('rows', 'tok'))]
    unnamed x14 -> x12, local copies, waits for them, and re-layouts: 21.7 us -> 19.5 us
  transfers between devices with their start and end apart: 2 -> 1, of which waited for: 2 -> 1; matrix products, arithmetic and copies ran while one was open for 0% -> 0% of each run, Pallas kernels for 0% -> 0%
where the time goes in v2:
time: 166 us
  Pallas kernels  112 us (67%)
  blocking collectives  30.2 us (18%)
  local copies, waits for them, and re-layouts  20 us (12%)
    pallas_call x1, Pallas kernels, summed(): pl.pallas_call(functools.partial(total_kernel, plan), out_shape=jax.Shape...  49 us
    pallas_call x1, Pallas kernels, make_projector(): pl.pallas_call(functools.partial(projector_kernel, noise_norm, pixel_tota...  31.3 us
    all_to_all x1, blocking collectives, local(): lax.all_to_all(outgoing, 'rows', split_axis=0, concat_axis=0, tiled=True)  30.2 us
    unnamed x12, local copies, waits for them, and re-layouts  19.5 us
    pallas_call x1, Pallas kernels, moments(): pl.pallas_call(moments_kernel, grid=(steps,), in_specs=[pl.BlockSpec((STE...  17 us
    pallas_call x1, Pallas kernels, project(): pl.pallas_call(project_kernel, grid=(steps,), in_specs=[pl.BlockSpec((STE...  14.4 us
  transfers between devices with their start and end apart: 1, of which 1 were waited for; matrix products, arithmetic and copies ran while one was open for 0% of the time, Pallas kernels for 0%

profile of v2, /device:TPU:0, one launch (start us, length us, event | category | flops | bytes accessed | tf_op | source)
XLA Modules:
  0.0 166.0 jit_solution(3277221677876654260)
XLA Ops:
  0.6 0.0 copy-start.2
  0.6 0.0 copy-start.3
  0.6 13.1 %copy.19.x_ref.ahead_ref = bf16[128,425,128]{2,1,0:T(8,128)(2,1)S(1)} copy(bf16[128,425,128]{2,0,1:T(8,128)(2,1)} %param.4) | data formatting | bytes 27852800 | tf_op args[0]
  13.8 0.0 copy-start
  13.8 5.0 %copy-done = bf16[128,425,128]{2,1,0:T(8,128)(2,1)} copy-done((bf16[128,425,128]{2,1,0:T(8,128)(2,1)}, bf16[128,425,128]{2,1,0:T(8,128)(2,1)S(1)}, u32[]{:S(2)}) %copy-start) | copy-done | bytes 13926424
  18.8 0.0 copy-start.1
  18.8 1.4 collective-permute-start
  20.3 0.0 copy-done.2
  20.3 0.1 eq.47
  20.4 0.0 copy-done.3
  20.4 0.1 compare_reduce_fusion
  20.5 0.2 fusion.5.spread_ref
  20.7 0.3 fusion.4
  21.0 0.1 mul.40
  21.1 0.0 copy-done.1
  21.1 1.1 collective-permute-done.halo_ref
  22.2 17.0 %moments.1 = (f32[2,432,256]{2,1,0:T(8,128)S(1)}, f32[2,176,176]{2,1,0:T(8,128)S(1)}, f32[432,1]{1,0:T(8,128)S(1)}) custom-call(bf16[128,425,128]{2,1,0:T(8,128)(2,1)} %copy-done, bf16[128,425,128]{2,1,0:T(8,128)(2,1)} %copy-done, bf16[1,425,128]{2,1,0:T(8,128)(2,1)S(1)} %collective-permute-done.halo_ref, s32[128]{0:T(128)S(1)} %and_convert_fusion.valid_ref), custom_call_target="tpu_custom_call" | custom-call | flops 11837440000 | bytes 13926400 | tf_op jit(solution)/shard_map/moments/pallas_call | solution.py:77
  39.2 0.1 reduce
  39.3 0.1 fusion.1
  39.4 0.1 pad.18.mine_ref
  39.5 49.0 %total.1 = f32[1280,256]{1,0:T(8,128)S(1)} custom-call(f32[1280,256]{1,0:T(8,128)S(1)} %pad.18.mine_ref), custom_call_target="tpu_custom_call" | custom-call | tf_op jit(solution)/shard_map/total/pallas_call | solution.py:193
  88.5 0.1 slice.16
  88.6 0.1 copy.18.band_ref
  88.7 31.3 %projector.1 = (bf16[64,432]{1,0:T(8,128)(2,1)S(1)}, f32[64,128]{1,0:T(8,128)S(1)}) custom-call(f32[2,432,256]{2,1,0:T(8,128)S(1)} %bitcast.13, f32[2,176,176]{2,1,0:T(8,128)S(1)} %bitcast.15, f32[432,1]{1,0:T(8,128)S(1)} %copy.18.band_ref, f32[64,512]{1,0:T(8,128)S(1)} %pad.19.start_ref), custom_call_target="tpu_custom_call" | custom-call | tf_op jit(solution)/shard_map/projector/pallas_call | solution.py:326
  120.0 14.4 %project.1 = (bf16[1024,1024]{1,0:T(8,128)(2,1)S(1)}, bf16[128,64,128]{2,1,0:T(8,128)(2,1)}) custom-call(bf16[128,425,128]{2,1,0:T(8,128)(2,1)} %copy-done, bf16[1,425,128]{2,1,0:T(8,128)(2,1)S(1)} %collective-permute-done.halo_ref, s32[128]{0:T(128)S(1)} %and_convert_fusion.valid_ref, bf16[64,432]{1,0:T(8,128)(2,1)S(1)} %get-tuple-element.12.proj_ref, ...), custom_call_target="tpu_custom_call" | custom-call | tf_op jit(solution)/shard_map/project/pallas_call | solution.py:420
  134.5 30.2 %all_to_all.5 = bf16[8,128,1024]{2,1,0:T(8,128)(2,1)S(1)} all-to-all(bf16[8,128,1024]{2,1,0:T(8,128)(2,1)S(1)} %bitcast.14), channel_id=1, replica_groups=mesh['rows'=8,'tok'=4] {'rows'}, dimensions={0} | all-to-all | bytes 4194304 | tf_op jit(solution)/shard_map/all_to_all | solution.py:482
  164.6 1.3 copy.22
  (13 shorter events, 0.1 us)
Async XLA Ops:
  0.6 19.7 %copy-start.2 = (s32[32,32]{1,0:T(8,128)S(1)}, s32[32,32]{1,0:T(8,128)}, u32[]{:S(2)}) copy-start(s32[32,32]{1,0:T(8,128)} %param.6) | copy-start | bytes 12292
  0.6 19.8 %copy-start.3 = (s32[4]{0:T(128)S(1)}, s32[4]{0:T(128)}, u32[]{:S(2)}) copy-start(s32[4]{0:T(128)} %param.5) | copy-start | bytes 52
  13.8 5.1 %copy-start = (bf16[128,425,128]{2,1,0:T(8,128)(2,1)}, bf16[128,425,128]{2,1,0:T(8,128)(2,1)S(1)}, u32[]{:S(2)}) copy-start(bf16[128,425,128]{2,1,0:T(8,128)(2,1)S(1)} %copy.19.x_ref.ahead_ref) | copy-start | bytes 41779204
  18.8 2.2 %copy-start.1 = (f32[425,64]{0,1:T(8,128)S(1)}, f32[425,64]{0,1:T(8,128)}, u32[]{:S(2)}) copy-start(f32[425,64]{0,1:T(8,128)} %param.7) | copy-start | bytes 326404
  18.8 3.3 %collective-permute-start = (bf16[1,425,128]{2,1,0:T(8,128)(2,1)S(1)}, bf16[1,425,128]{2,1,0:T(8,128)(2,1)S(1)}, u32[]{:S(2)}, u32[]{:S(2)}) collective-permute-start(bf16[1,425,128]{2,1,0:T(8,128)(2,1)S(1)} %slice.20), channel_id=1, source_target_pairs={{4,0},{8,4},{12,8},{16,12},{20,16},{24,20},{28,24},{5,1},{9,5},{13... | collective-permute-start | bytes 326408 | tf_op jit(solution)/shard_map/ppermute | solution.py:26

commit v3 on v2

--- a/solution.py
+++ b/solution.py
@@ -98,7 +98,7 @@
             pltpu.VMEM((tall, STEP * cols), BF16),
             pltpu.VMEM((bands, cols), F32),
         ],
-        compiler_params=pltpu.CompilerParams(vmem_limit_bytes=48 * 2**20),
+        compiler_params=pltpu.CompilerParams(vmem_limit_bytes=58 * 2**20),
         cost_estimate=pl.CostEstimate(
             flops=4 * local_rows * cols * bands * bands,
             bytes_accessed=2 * local_rows * cols * bands,
@@ -330,7 +330,7 @@
             jax.ShapeDtypeStruct((comps, 128), F32),
         ],
         scratch_shapes=[pltpu.VMEM((size, size), F32)] + [square] * 8,
-        compiler_params=pltpu.CompilerParams(vmem_limit_bytes=48 * 2**20),
+        compiler_params=pltpu.CompilerParams(vmem_limit_bytes=58 * 2**20),
         name="projector",
     )(wide, tail, band, jnp.pad(start, ((0, 0), (0, size - start.shape[1]))))
 
@@ -441,7 +441,7 @@
             pltpu.VMEM((comps, cols), F32),
             pltpu.VMEM((patch_count, width), BF16),
         ],
-        compiler_params=pltpu.CompilerParams(vmem_limit_bytes=48 * 2**20),
+        compiler_params=pltpu.CompilerParams(vmem_limit_bytes=58 * 2**20),
         name="project",
     )(pixels, halo, valid, projector, offset, place, spread)
 

time: 166 us -> 176 us (1.060)
  other arithmetic: 0.51 us -> 4.69 us
  local copies, waits for them, and re-layouts: 20 us -> 23.7 us
  Pallas kernels: 112 us -> 114 us
    pallas_call x1, Pallas kernels: 31.3 us -> 33.2 us  [make_projector(): pl.pallas_call(functools.partial(projector_kernel, noise_norm, pixel_tota...]
    unnamed x12 -> x14, local copies, waits for them, and re-layouts: 19.5 us -> 20.2 us
  transfers between devices with their start and end apart: 1 -> 1, of which waited for: 1 -> 0; matrix products, arithmetic and copies ran while one was open for 0% -> 2% of each run, Pallas kernels for 0% -> 0%
where the time goes in v3:
time: 176 us; the launch traced here: 175 us
  Pallas kernels  114 us (65%)
  blocking collectives  30.4 us (17%)
  local copies, waits for them, and re-layouts  23.7 us (13%)
  other arithmetic  4.69 us (3%)
    pallas_call x1, Pallas kernels, summed(): pl.pallas_call(functools.partial(total_kernel, plan), out_shape=jax.Shape...  47.7 us
    pallas_call x1, Pallas kernels, make_projector(): pl.pallas_call(functools.partial(projector_kernel, noise_norm, pixel_tota...  33.2 us
    all_to_all x1, blocking collectives, local(): lax.all_to_all(outgoing, 'rows', split_axis=0, concat_axis=0, tiled=True)  30.4 us
    unnamed x14, local copies, waits for them, and re-layouts  20.2 us
    pallas_call x1, Pallas kernels, moments(): pl.pallas_call(moments_kernel, grid=(steps,), in_specs=[pl.BlockSpec((STE...  18 us
    pallas_call x1, Pallas kernels, project(): pl.pallas_call(project_kernel, grid=(steps,), in_specs=[pl.BlockSpec((STE...  15.3 us
  transfers between devices with their start and end apart: 1, of which 0 were waited for; matrix products, arithmetic and copies ran while one was open for 2% of the time, Pallas kernels for 0%

profile of v3, /device:TPU:0, one launch (start us, length us, event | category | flops | bytes accessed | tf_op | source)
XLA Modules:
  0.0 175.4 jit_solution(16882194470848024284)
XLA Ops:
  0.6 0.0 copy-start.3
  0.6 0.0 copy-start.4
  0.6 13.1 %copy.19.x_ref.ahead_ref = bf16[128,425,128]{2,1,0:T(8,128)(2,1)S(1)} copy(bf16[128,425,128]{2,0,1:T(8,128)(2,1)} %param.4) | data formatting | bytes 27852800 | tf_op args[0]
  13.8 0.0 copy-start
  13.8 5.1 %copy-done = bf16[128,425,128]{2,1,0:T(8,128)(2,1)} copy-done((bf16[128,425,128]{2,1,0:T(8,128)(2,1)}, bf16[128,425,128]{2,1,0:T(8,128)(2,1)S(1)}, u32[]{:S(2)}) %copy-start) | copy-done | bytes 13926424
  18.8 0.0 copy-start.1
  18.9 1.4 collective-permute-start
  20.3 0.0 copy-done.3
  20.3 0.1 eq.47
  20.4 0.0 copy-done.4
  20.4 0.1 compare_reduce_fusion
  20.5 0.6 and_convert_fusion.valid_ref
  21.1 0.9 fusion.5.spread_ref
  22.0 0.3 fusion.4
  22.4 0.1 mul.40
  22.4 0.6 add.84.place_ref
  23.0 0.0 copy-done.1
  23.0 0.7 pad.19.start_ref
  23.7 0.0 collective-permute-done.halo_ref
  23.7 0.0 copy-start.2
  23.7 0.6 copy-done.2
  24.4 18.0 %moments.1 = (f32[2,432,256]{2,1,0:T(8,128)}, f32[2,176,176]{2,1,0:T(8,128)}, f32[432,1]{1,0:T(8,128)}) custom-call(bf16[128,425,128]{2,1,0:T(8,128)(2,1)} %copy-done, bf16[128,425,128]{2,1,0:T(8,128)(2,1)} %copy-done, bf16[1,425,128]{2,1,0:T(8,128)(2,1)} %copy-done.2, s32[128]{0:T(128)} %and_convert_fusion.valid_ref), custom_call_target="tpu_custom_call" | custom-call | flops 11837440000 | bytes 13926400 | tf_op jit(solution)/shard_map/moments/pallas_call | solution.py:77
  42.4 1.1 reduce
  43.5 1.4 fusion.1
  44.8 0.1 pad.18.mine_ref
  44.9 47.7 %total.1 = f32[1280,256]{1,0:T(8,128)S(1)} custom-call(f32[1280,256]{1,0:T(8,128)S(1)} %pad.18.mine_ref), custom_call_target="tpu_custom_call" | custom-call | tf_op jit(solution)/shard_map/total/pallas_call | solution.py:193
  92.7 0.8 slice.17
  93.4 1.0 slice.16
  94.4 0.8 copy.18.band_ref
  95.2 33.2 %projector.1 = (bf16[64,432]{1,0:T(8,128)(2,1)}, f32[64,128]{1,0:T(8,128)}) custom-call(f32[2,432,256]{2,1,0:T(8,128)} %bitcast.14, f32[2,176,176]{2,1,0:T(8,128)} %bitcast.16, f32[432,1]{1,0:T(8,128)} %copy.18.band_ref, f32[64,512]{1,0:T(8,128)} %pad.19.start_ref), custom_call_target="tpu_custom_call" | custom-call | tf_op jit(solution)/shard_map/projector/pallas_call | solution.py:326
  128.4 15.3 %project.1 = (bf16[1024,1024]{1,0:T(8,128)(2,1)}, bf16[128,64,128]{2,1,0:T(8,128)(2,1)}) custom-call(bf16[128,425,128]{2,1,0:T(8,128)(2,1)} %copy-done, bf16[1,425,128]{2,1,0:T(8,128)(2,1)} %copy-done.2, s32[128]{0:T(128)} %and_convert_fusion.valid_ref, bf16[64,432]{1,0:T(8,128)(2,1)} %get-tuple-element.12.proj_ref, f32[64,128]{1,0:T(8,128)} %get-tuple-element.13.offset_ref, ...), custom_call_target="tpu_custom_call" | custom-call | tf_op jit(solution)/shard_map/project/pallas_call | solution.py:420
  143.7 30.4 %all_to_all.5 = bf16[8,128,1024]{2,1,0:T(8,128)(2,1)S(1)} all-to-all(bf16[8,128,1024]{2,1,0:T(8,128)(2,1)} %bitcast.15), channel_id=1, replica_groups=mesh['rows'=8,'tok'=4] {'rows'}, dimensions={0} | all-to-all | bytes 4194304 | tf_op jit(solution)/shard_map/all_to_all | solution.py:482
  174.1 1.3 copy.22
  (9 shorter events, 0.1 us)
Async XLA Ops:
  0.6 19.7 %copy-start.3 = (s32[32,32]{1,0:T(8,128)S(1)}, s32[32,32]{1,0:T(8,128)}, u32[]{:S(2)}) copy-start(s32[32,32]{1,0:T(8,128)} %param.6) | copy-start | bytes 12292
  0.6 19.8 %copy-start.4 = (s32[4]{0:T(128)S(1)}, s32[4]{0:T(128)}, u32[]{:S(2)}) copy-start(s32[4]{0:T(128)} %param.5) | copy-start | bytes 52
  13.8 5.1 %copy-start = (bf16[128,425,128]{2,1,0:T(8,128)(2,1)}, bf16[128,425,128]{2,1,0:T(8,128)(2,1)S(1)}, u32[]{:S(2)}) copy-start(bf16[128,425,128]{2,1,0:T(8,128)(2,1)S(1)} %copy.19.x_ref.ahead_ref) | copy-start | bytes 41779204
  18.8 4.2 %copy-start.1 = (f32[425,64]{0,1:T(8,128)S(1)}, f32[425,64]{0,1:T(8,128)}, u32[]{:S(2)}) copy-start(f32[425,64]{0,1:T(8,128)} %param.7) | copy-start | bytes 326404
  18.9 4.9 %collective-permute-start = (bf16[1,425,128]{2,1,0:T(8,128)(2,1)S(1)}, bf16[1,425,128]{2,1,0:T(8,128)(2,1)S(1)}, u32[]{:S(2)}, u32[]{:S(2)}) collective-permute-start(bf16[1,425,128]{2,1,0:T(8,128)(2,1)S(1)} %slice.20), channel_id=1, source_target_pairs={{4,0},{8,4},{12,8},{16,12},{20,16},{24,20},{28,24},{5,1},{9,5},{13... | collective-permute-start | bytes 326408 | tf_op jit(solution)/shard_map/ppermute | solution.py:26
  23.7 0.6 copy-start.2
